TPU v7x, 256 devices: a whole 4x4x8 slice. The times are simulated.
256 devices in a mesh: terms: 64 (over x, z_lo, y, core), rows: 4 (over z_hi).
Axes of the slice: x: 4, y: 4, z: 8 (z_hi: 4, z_lo: 2; z = z_hi * 2 + z_lo), core: 2. Of those that a mesh axis runs over, the one named last changes fastest.
Arguments:
- amplitudes: float32 [768, 768], P('rows'), may hold values from -6 to 6
- left_terms: float32 [64, 768, 768], P('terms', 'rows'), may hold values from -0.02734375 to 0.02734375
- right_terms: float32 [64, 768, 768], P('terms'), may hold values from -0.21875 to 0.21875
- source_list: int32 [64, 4], replicated, may hold values from 0 to 63, as said below
- list_count: int32 [64], replicated, may hold values from 1 to 4
- weight_index: int32 [64, 4], replicated, may hold values from 0 to 7
- weight_table: float32 [8], replicated, may hold values from -4 to 4
Outputs:
- isometry: float32 [768, 768], P('rows')
- new_environment: float32 [64, 768, 768], P('terms', 'rows')
Inputs may be any that keep to these rules, and one draw needn't show every extreme that they name: `source_list`: every block id appears in column 0 exactly once.
All inputs are finite; a program needn't handle non-finite values.
Results may differ from a plain program's by a relative error of at most 0.00016.
Values sent between devices are 32-bit elements; how exact they have to be, the bound alone decides.
A program may use at most 64 MiB of HBM per device.

v0:
```python
import math

import jax
import jax.numpy as jnp
from jax import lax
from jax.sharding import PartitionSpec as P

K = 768
FAN = 4
SWEEPS = 3


HIGH = lax.Precision.HIGHEST
COEF_ONE = 3.4445
COEF_TWO = -4.775
COEF_THREE = 2.0315


def fold_rows(left_terms, piece):
    return jnp.einsum(
        "trk,kc->trc", left_terms, piece, precision=HIGH, preferred_element_type=jnp.float32
    )


def apply_terms(amplitudes, left_terms, right_terms):
    mapped = fold_rows(left_terms, lax.all_gather(amplitudes, "rows", axis=0, tiled=True))
    partial_sum = jnp.einsum(
        "trc,tcd->rd", mapped, right_terms, precision=HIGH, preferred_element_type=jnp.float32
    )
    summed = lax.psum(partial_sum, "terms")
    return amplitudes - 0.3 * summed


def gram_full(matrix):
    gram_part = jnp.dot(matrix.T, matrix, precision=HIGH, preferred_element_type=jnp.float32)
    shared = lax.psum_scatter(gram_part, "rows", scatter_dimension=1, tiled=True)
    gram_matrix = lax.all_gather(shared, "rows", axis=1, tiled=True)
    return gram_matrix


def schulz_update(iterate, gram_matrix):
    once = jnp.dot(iterate, gram_matrix, precision=HIGH, preferred_element_type=jnp.float32)
    twice = jnp.dot(once, gram_matrix, precision=HIGH, preferred_element_type=jnp.float32)
    return COEF_ONE * iterate + COEF_TWO * once + COEF_THREE * twice


def combination(source_list, list_count, weight_index, weight_table):
    block_count = source_list.shape[0]
    table_size = weight_table.shape[0]
    in_use = (jnp.arange(FAN)[None, :] < list_count[:, None]).astype(jnp.float32)
    picked = (weight_index[:, :, None] == jnp.arange(table_size)[None, None, :]).astype(jnp.float32)
    weights = jnp.einsum("jcn,n->jc", picked, weight_table, precision=HIGH) * in_use
    matches = (source_list[:, :, None] == jnp.arange(block_count)[None, None, :]).astype(
        jnp.float32
    )
    return jnp.einsum("jc,jcb->jb", weights, matches, precision=HIGH)


def body(amplitudes, left_terms, right_terms, source_list, list_count, weight_index, weight_table):
    first = apply_terms(amplitudes, left_terms, right_terms)
    second = apply_terms(first, left_terms, right_terms)
    squares = lax.psum(jnp.sum(second * second), "rows")
    iterate = second / jnp.sqrt(squares)
    for repeat in range(SWEEPS):
        iterate = schulz_update(iterate, gram_full(iterate))
    isometry = math.sqrt(K) * iterate
    terms_here = left_terms.shape[0]
    rows_here = left_terms.shape[1]
    width = left_terms.shape[2]
    owners = lax.axis_size("terms")
    run_length = rows_here * width // owners
    flat_blocks = left_terms.reshape(terms_here, owners, run_length)
    pieces = lax.all_to_all(flat_blocks, "terms", split_axis=1, concat_axis=0, tiled=True)
    pieces = pieces.reshape(terms_here * owners, run_length)
    mixing = combination(source_list, list_count, weight_index, weight_table)
    combined = jnp.dot(mixing, pieces, precision=HIGH, preferred_element_type=jnp.float32)
    combined = combined.reshape(terms_here * owners, 1, run_length)
    owned = lax.all_to_all(combined, "terms", split_axis=0, concat_axis=1, tiled=True)
    owned = owned.reshape(terms_here, rows_here, width)
    whole_isometry = lax.all_gather(isometry, "rows", axis=0, tiled=True)
    rotated = jnp.einsum(
        "trk,kd->trd", owned, whole_isometry, precision=HIGH, preferred_element_type=jnp.float32
    )
    projected = lax.psum_scatter(
        jnp.einsum(
            "ri,trd->itd", isometry, rotated, precision=HIGH, preferred_element_type=jnp.float32
        ),
        "rows",
        scatter_dimension=0,
        tiled=True,
    )
    new_environment = jnp.transpose(projected, (1, 0, 2))
    return (isometry, new_environment)


def solution(mesh):
    placed = (P("rows", None), P("terms", "rows", None), P("terms", None, None), P(), P(), P(), P())
    return jax.shard_map(
        body,
        mesh=mesh,
        in_specs=placed,
        out_specs=(P("rows", None), P("terms", "rows", None)),
        check_vma=False,
    )
```

profile of v0, /device:TPU:1, one launch (start us, length us, event | category | flops | bytes accessed | tf_op | source)
XLA Modules:
  0.0 1672.7 jit_solution(1284039506310649906)
XLA Ops:
  8.0 61.7 %all-gather.7.cloned.1.call-done = f32[768,768]{1,0:T(8,128)} async-done(((f32[192,768]{1,0:T(8,128)}), f32[768,768]{1,0:T(8,128)}) %all-gather.7.cloned.1.call-update) | async-done | bytes 2359312 | tf_op jit(solution)/shard_map/all_gather | solution.py:26
  69.7 3.6 fusion.12
  76.0 511.7 %all-reduce.3.cloned.1.call-done = f32[192,768]{1,0:T(8,128)} async-done(((f32[192,768]{1,0:T(8,128)}), f32[192,768]{1,0:T(8,128)}) %all-reduce.3.cloned.1.call-update) | async-done | bytes 589840 | tf_op jit(solution)/shard_map/psum | solution.py:30
  589.7 55.3 %all-gather.9.cloned.1.call-done = f32[768,768]{1,0:T(8,128)} async-done(((f32[192,768]{1,0:T(8,128)}), f32[768,768]{1,0:T(8,128)}) %all-gather.9.cloned.1.call-update) | async-done | bytes 2359312 | tf_op jit(solution)/shard_map/all_gather | solution.py:26
  645.0 5.5 fusion.10
  653.4 511.7 %all-reduce.5.cloned.1.call-done = f32[192,768]{1,0:T(8,128)} async-done(((f32[192,768]{1,0:T(8,128)}), f32[192,768]{1,0:T(8,128)}) %all-reduce.5.cloned.1.call-update) | async-done | bytes 589840 | tf_op jit(solution)/shard_map/psum | solution.py:30
  1166.9 10.7 psum.23
  1179.4 3.5 fusion.18
  1183.4 52.1 %reduce-scatter.5.cloned.1.call-done = f32[768,192]{0,1:T(8,128)} async-done(((f32[768,768]{0,1:T(8,128)}), f32[768,192]{0,1:T(8,128)}) %reduce-scatter.5.cloned.1.call-update) | async-done | bytes 589840 | tf_op jit(solution)/shard_map/reduce_scatter | solution.py:36
  1235.6 55.9 %all-gather.11.cloned.1.call-done = f32[768,768]{0,1:T(8,128)} async-done(((f32[768,192]{0,1:T(8,128)}), f32[768,768]{0,1:T(8,128)}) %all-gather.11.cloned.1.call-update) | async-done | bytes 2359312 | tf_op jit(solution)/shard_map/all_gather | solution.py:37
  1291.5 4.3 fusion.19
  1298.3 3.5 fusion.20
  1301.9 53.2 %reduce-scatter.7.cloned.1.call-done = f32[768,192]{0,1:T(8,128)} async-done(((f32[768,768]{0,1:T(8,128)}), f32[768,192]{0,1:T(8,128)}) %reduce-scatter.7.cloned.1.call-update) | async-done | bytes 589840 | tf_op jit(solution)/shard_map/reduce_scatter | solution.py:36
  1355.2 56.0 %all-gather.13.cloned.1.call-done = f32[768,768]{0,1:T(8,128)} async-done(((f32[768,192]{0,1:T(8,128)}), f32[768,768]{0,1:T(8,128)}) %all-gather.13.cloned.1.call-update) | async-done | bytes 2359312 | tf_op jit(solution)/shard_map/all_gather | solution.py:37
  1411.2 4.3 fusion.21
  1418.1 3.5 fusion.22
  1421.7 53.2 %reduce-scatter.9.cloned.1.call-done = f32[768,192]{0,1:T(8,128)} async-done(((f32[768,768]{0,1:T(8,128)}), f32[768,192]{0,1:T(8,128)}) %reduce-scatter.9.cloned.1.call-update) | async-done | bytes 589840 | tf_op jit(solution)/shard_map/reduce_scatter | solution.py:36
  1475.0 55.9 %all-gather.15.cloned.1.call-done = f32[768,768]{0,1:T(8,128)} async-done(((f32[768,192]{0,1:T(8,128)}), f32[768,768]{0,1:T(8,128)}) %all-gather.15.cloned.1.call-update) | async-done | bytes 2359312 | tf_op jit(solution)/shard_map/all_gather | solution.py:37
  1530.9 4.3 fusion.23
  1540.0 8.8 all-to-all-start
  1549.8 25.3 %all-to-all-done = f32[1,64,2304]{2,0,1:T(1,128)S(1)} async-done(((f32[1,64,2304]{2,0,1:T(1,128)}), f32[1,64,2304]{2,0,1:T(1,128)S(1)}, u32[]{:S(2)}, u32[]{:S(2)}) %all-to-all-start) | async-done | bytes 589856 | tf_op jit(solution)/shard_map/all_to_all | solution.py:73
  1576.3 30.0 %all_to_all.8 = f32[64,1,2304]{2,1,0:T(1,128)S(1)} all-to-all(f32[64,1,2304]{2,1,0:T(1,128)S(1)} %copy.13), channel_id=1, replica_groups=mesh['terms'=64,'rows'=4] {'terms'}, dimensions={0} | all-to-all | bytes 1179648 | tf_op jit(solution)/shard_map/all_to_all | solution.py:78
  1613.3 3.5 convolution_bitcast_fusion.1
  1616.9 48.8 %reduce-scatter.11.cloned.1.call-done = f32[192,1,768]{2,0,1:T(8,128)} async-done(((f32[768,1,768]{2,0,1:T(8,128)}), f32[192,1,768]{2,0,1:T(8,128)}) %reduce-scatter.11.cloned.1.call-update) | async-done | bytes 589840 | tf_op jit(solution)/shard_map/reduce_scatter | solution.py:84
  (70 shorter events, 31.0 us)
Async XLA Ops:
  7.2 66.2 %copy-start = (f32[1,768,768]{2,1,0:T(8,128)S(1)}, f32[1,768,768]{2,1,0:T(8,128)}, u32[]{:S(2)}) copy-start(f32[1,768,768]{2,1,0:T(8,128)} %param.9) | copy-start | bytes 7077892
  7.2 62.5 %all-gather.7.cloned.1.call-start = ((), (), s32[]{:S(2)}) async-start(), calls=%async_computation.6 | async-start | bytes 2949120 | tf_op jit(solution)/shard_map/all_gather | solution.py:26
  7.9 579.8 %all-reduce.3.cloned.1.call-start = ((), (), s32[]{:S(2)}) async-start(), calls=%async_computation.7 | async-start | bytes 1179648 | tf_op jit(solution)/shard_map/psum | solution.py:30
  73.3 514.4 %copy-start.8 = (f32[192,768]{1,0:T(8,128)S(1)}, f32[192,768]{1,0:T(8,128)}, u32[]{:S(2)}) copy-start(f32[192,768]{1,0:T(8,128)} %param.7) | copy-start | bytes 1769476
  75.9 569.1 %copy-start.5 = (f32[1,192,768]{2,1,0:T(8,128)S(1)}, f32[1,192,768]{2,1,0:T(8,128)}, u32[]{:S(2)}) copy-start(f32[1,192,768]{2,1,0:T(8,128)} %param.8) | copy-start | bytes 1769476
  75.9 569.1 %all-gather.9.cloned.1.call-start = ((), (), s32[]{:S(2)}) async-start(), calls=%async_computation.8 | async-start | bytes 2949120 | tf_op jit(solution)/shard_map/all_gather | solution.py:26
  589.7 575.4 %all-reduce.5.cloned.1.call-start = ((), (), s32[]{:S(2)}) async-start(), calls=%async_computation.9 | async-start | bytes 1179648 | tf_op jit(solution)/shard_map/psum | solution.py:30
  650.5 514.6 %copy-start.4 = (f32[192,768]{1,0:T(8,128)S(1)}, f32[192,768]{1,0:T(8,128)}, u32[]{:S(2)}) copy-start(f32[192,768]{1,0:T(8,128)} %multiply_subtract_fusion.1) | copy-start | bytes 1769476
  653.3 582.2 %reduce-scatter.5.cloned.1.call-start = ((), (), s32[]{:S(2)}) async-start(), calls=%async_computation.10 | async-start | bytes 2949120 | tf_op jit(solution)/shard_map/reduce_scatter | solution.py:36
  1183.0 108.5 %all-gather.11.cloned.1.call-start = ((), (), s32[]{:S(2)}) async-start(), calls=%async_computation.11 | async-start | bytes 2949120 | tf_op jit(solution)/shard_map/all_gather | solution.py:37
  1235.5 119.6 %reduce-scatter.7.cloned.1.call-start = ((), (), s32[]{:S(2)}) async-start(), calls=%async_computation.12 | async-start | bytes 2949120 | tf_op jit(solution)/shard_map/reduce_scatter | solution.py:36
  1291.5 4.3 copy-start.1
  1301.9 109.4 %all-gather.13.cloned.1.call-start = ((), (), s32[]{:S(2)}) async-start(), calls=%async_computation.13 | async-start | bytes 2949120 | tf_op jit(solution)/shard_map/all_gather | solution.py:37
  1355.1 119.7 %reduce-scatter.9.cloned.1.call-start = ((), (), s32[]{:S(2)}) async-start(), calls=%async_computation.14 | async-start | bytes 2949120 | tf_op jit(solution)/shard_map/reduce_scatter | solution.py:36
  1411.2 4.3 copy-start.2
  1421.6 109.2 %all-gather.15.cloned.1.call-start = ((), (), s32[]{:S(2)}) async-start(), calls=%async_computation.15 | async-start | bytes 2949120 | tf_op jit(solution)/shard_map/all_gather | solution.py:37
  1474.9 135.0 %all-gather.17.cloned.1.call-start = ((), (), s32[]{:S(2)}) async-start(), calls=%async_computation.16 | async-start | bytes 2949120 | tf_op jit(solution)/shard_map/all_gather | solution.py:80
  1538.5 10.3 copy-start.9
  1538.5 10.4 copy-start.10
  1538.5 10.5 copy-start.11
  1538.5 10.8 copy-start.12
  1540.0 35.1 %all-to-all-start = ((f32[1,64,2304]{2,0,1:T(1,128)}), f32[1,64,2304]{2,0,1:T(1,128)S(1)}, u32[]{:S(2)}, u32[]{:S(2)}) async-start(f32[1,64,2304]{2,0,1:T(1,128)} %reshape.49), calls=%async_computation.3 | async-start | bytes 1179648 | tf_op jit(solution)/shard_map/all_to_all | solution.py:73
  1548.8 116.9 %reduce-scatter.11.cloned.1.call-start = ((), (), s32[]{:S(2)}) async-start(), calls=%async_computation.17 | async-start | bytes 2949120 | tf_op jit(solution)/shard_map/reduce_scatter | solution.py:84
  1608.6 4.7 copy-start.7
  (2 other events, 7.7 us)
Sparse Core Ops, SparseCore 0:
  9.8 59.8 all-gather.6
  76.0 511.5 all-reduce.2
  590.2 54.7 all-gather.8
  653.4 511.6 all-reduce.4
  1183.1 52.3 reduce-scatter.4
  1237.2 54.2 all-gather.10
  1302.0 53.0 reduce-scatter.6
  1356.9 54.2 all-gather.12
  1421.7 53.0 reduce-scatter.8
  1476.5 54.2 all-gather.14
  1538.7 63.3 all-gather.16
  1617.0 48.6 reduce-scatter.10
where the time goes:
time: 1680 us; the launch traced here: 1670 us
  waiting for transfers between devices  1540 us (92%)
  matrix products  54.3 us (3%)
  blocking collectives  40.7 us (2%)
    psum x2, waiting for transfers between devices, apply_terms(): summed = lax.psum(partial_sum, 'terms')  1020 us
    all_gather x3, waiting for transfers between devices, gram_full(): gram_matrix = lax.all_gather(shared, 'rows', axis=1, tiled=True)  168 us
    reduce_scatter x3, waiting for transfers between devices, gram_full(): lax.psum_scatter(gram_part, 'rows', scatter_dimension=1, tiled=True)  159 us
    all_gather x2, waiting for transfers between devices, apply_terms(): lax.all_gather(amplitudes, 'rows', axis=0, tiled=True)  117 us
    reduce_scatter x1, waiting for transfers between devices, body(): lax.psum_scatter(jnp.einsum('ri,trd->itd', isometry, rotated, precision=H...  48.8 us
  transfers between devices with their start and end apart: 13, of which 12 were waited for; matrix products, arithmetic and copies ran while one was open for 0% of the time, Pallas kernels for 0%

commit v1 on v0

v1 whole, which is shorter than its diff:
```python
import math

import jax
import jax.numpy as jnp
from jax import lax
from jax.experimental import pallas as pl
from jax.experimental.pallas import tpu as pltpu
from jax.sharding import PartitionSpec as P

K = 768
FAN = 4
SWEEPS = 3
SLAB = 192
OWNERS = 48
TR, TC = 8, 384
COEF_ONE = 3.4445
COEF_TWO = -4.775
COEF_THREE = 2.0315
MESH = pl.DeviceIdType.MESH
BF = jnp.bfloat16
F32 = jnp.float32


def halves(value):
    high = value.astype(BF)
    return high, (value - high.astype(F32)).astype(BF)


def split(src, high, low, rows, step):
    @pl.loop(0, rows // step)
    def _(i):
        at = pl.ds(pl.multiple_of(i * step, step), step)
        high[at, :], low[at, :] = halves(src[at, :])


def product(ah, al, bh, bl, cols):
    left_h, left_l = ah, al
    rh, rl = bh[:, cols], bl[:, cols]
    return jnp.dot(
        jnp.concatenate([left_h, left_h, left_l], axis=1),
        jnp.concatenate([rh, rl, rh], axis=0),
        preferred_element_type=F32,
    )


def wait(ref, sem):
    pltpu.make_async_copy(ref, ref, sem).wait()


def kernel(
    a_ref, l_ref, r_ref, source, count, windex, wtable,
    iso_ref, env_ref,
    lh, ll, rh, rl, xh, xl, yh, yl, uh, ul, part, x, g, w,
    ga, rs, mine, cb, co, cf,
    z_send, z_recv, s1_send, s1_recv, s2_send, s2_recv, sib_send, sib_recv,
    rs_send, rs_recv, c1_send, c1_recv, c2_send, c2_recv, c3_send, c3_recv,
):
    t = lax.axis_index("terms")
    r = lax.axis_index("rows")
    core = t % 2
    cy = (t // 2) % 4
    zl = (t // 8) % 2
    cx = t // 16
    pos = cx * 4 + cy
    dq = zl * 2 + core
    q = jnp.where(pos % 2 == 1, 3 - dq, dq)
    is_owner = q < 3
    own = jnp.minimum(pos * 3 + q, OWNERS - 1)

    def term(xx, zz, yy, cc):
        return ((xx * 2 + zz) * 4 + yy) * 2 + cc

    def owner_term(m):
        p = m // 3
        qq = m % 3
        d = jnp.where(p % 2 == 1, 3 - qq, qq)
        return term(p // 4, d // 2, p % 4, d % 2)

    def chunk(ref, m, row0=0):
        rows = pl.ds(pl.multiple_of(row0 + (m // 2) * TR, TR), TR)
        return ref.at[rows, pl.ds(pl.multiple_of((m % 2) * TC, TC), TC)]

    def there(tt, rr):
        return {"terms": tt, "rows": rr}

    def remote(src, dst, send, recv, tt, rr):
        return pltpu.make_async_remote_copy(
            src_ref=src, dst_ref=dst, send_sem=send, recv_sem=recv,
            device_id=there(tt, rr), device_id_type=MESH,
        )

    barrier = pltpu.get_barrier_semaphore()

    @pl.loop(1, 64)
    def _(i):
        pl.semaphore_signal(barrier, inc=1, device_id=there((t + i) % 64, r), device_id_type=MESH)

    for dr in range(1, 4):
        for zz in range(2):
            for cc in range(2):
                pl.semaphore_signal(
                    barrier, inc=1, device_id=there(term(cx, zz, cy, cc), (r + dr) % 4), device_id_type=MESH
                )
    pl.semaphore_wait(barrier, 75)

    def to_owners(src, dst, send, recv):
        @pl.loop(0, OWNERS)
        def _(i):
            m = (i + own) % OWNERS
            o = owner_term(m)
            slot = (t - o + 63) % 64

            @pl.when(o != t)
            def _():
                remote(chunk(src, m), dst.at[slot], send, recv, o, r).start()

        @pl.when(is_owner)
        def _():
            dst[63] = chunk(src, own)[...]

    def to_owners_sent(send):
        @pl.when(is_owner)
        def _():
            wait(cb.at[pl.ds(0, 47)], send)

        @pl.when(jnp.logical_not(is_owner))
        def _():
            wait(cb.at[pl.ds(0, 48)], send)

    side_b = jnp.where(core == 0, cx, cy)
    side_a = jnp.where(core == 0, cy, cx)
    here = side_b * 4 + side_a
    right, left, opposite = (side_b + 1) % 4, (side_b + 3) % 4, (side_b + 2) % 4
    kk = 4 * jnp.minimum(q, 2) + r
    to_core = kk // 6
    to_slot = kk % 6
    to_pos = jnp.where(to_core == 0, cx * 4 + cy, cy * 4 + cx)

    def partner(bb, aa):
        return term(jnp.where(core == 0, bb, aa), zl, jnp.where(core == 0, aa, bb), core)

    sibling = term(cx, zl, cy, 1 - core)

    def half(f, cc, bb, hh):
        return ga.at[f, cc, pl.ds(bb * 4 + 2 * hh, 2)]

    def gather_start(f):
        @pl.when(is_owner)
        def _():
            for dz in range(2):
                for dr in range(4):
                    tt, rr = term(cx, (zl + dz) % 2, cy, to_core), (r + dr) % 4
                    dst = ga.at[f, to_core, to_pos, to_slot]
                    if dz == 0 and dr == 0:
                        @pl.when(to_core == core)
                        def _():
                            pltpu.make_async_copy(mine.at[f], dst, z_recv.at[f, to_slot]).start()

                        @pl.when(to_core != core)
                        def _():
                            remote(mine.at[f], dst, z_send.at[f], z_recv.at[f, to_slot], tt, rr).start()
                    else:
                        remote(mine.at[f], dst, z_send.at[f], z_recv.at[f, to_slot], tt, rr).start()

    def gather_rest(f):
        for i in range(6):
            wait(ga.at[f, core, here, i], z_recv.at[f, i])
        block = ga.at[f, core, here]
        for d in range(1, 4):
            remote(block, block, s1_send.at[f], s1_recv.at[f, d - 1], partner(side_b, (side_a + d) % 4), r).start()
        for d in range(1, 4):
            wait(ga.at[f, core, side_b * 4 + (side_a + 4 - d) % 4], s1_recv.at[f, d - 1])

        def push(src, tt, sem):
            remote(src, src, s2_send.at[f], s2_recv.at[f, sem], tt, r).start()

        def across(src, sem):
            remote(src, src, sib_send.at[f], sib_recv.at[f, sem], sibling, r).start()

        to_right, to_left = partner(right, side_a), partner(left, side_a)
        push(half(f, core, side_b, 0), to_right, 0)
        push(half(f, core, side_b, 1), to_left, 2)
        push(half(f, core, side_b, 1), to_right, 1)
        push(half(f, core, side_b, 0), to_left, 3)
        across(ga.at[f, core, pl.ds(side_b * 4, 4)], 0)
        wait(half(f, core, left, 0), s2_recv.at[f, 0])
        push(half(f, core, left, 0), to_right, 4)
        wait(half(f, core, right, 1), s2_recv.at[f, 2])
        push(half(f, core, right, 1), to_left, 5)
        across(half(f, core, left, 0), 1)
        across(half(f, core, right, 1), 2)
        wait(half(f, core, left, 1), s2_recv.at[f, 1])
        across(half(f, core, left, 1), 3)
        wait(half(f, core, right, 0), s2_recv.at[f, 3])
        across(half(f, core, right, 0), 4)
        wait(half(f, core, opposite, 0), s2_recv.at[f, 4])
        across(half(f, core, opposite, 0), 5)
        wait(half(f, core, opposite, 1), s2_recv.at[f, 5])
        across(half(f, core, opposite, 1), 6)
        sb = side_a
        sr, sl, so = (sb + 1) % 4, (sb + 3) % 4, (sb + 2) % 4
        oc = 1 - core
        wait(ga.at[f, oc, pl.ds(sb * 4, 4)], sib_recv.at[f, 0])
        wait(half(f, oc, sl, 0), sib_recv.at[f, 1])
        wait(half(f, oc, sr, 1), sib_recv.at[f, 2])
        wait(half(f, oc, sl, 1), sib_recv.at[f, 3])
        wait(half(f, oc, sr, 0), sib_recv.at[f, 4])
        wait(half(f, oc, so, 0), sib_recv.at[f, 5])
        wait(half(f, oc, so, 1), sib_recv.at[f, 6])

    def gather_sent(f):
        @pl.when(is_owner)
        def _():
            @pl.when(to_core == core)
            def _():
                wait(cb.at[pl.ds(0, 7)], z_send.at[f])

            @pl.when(to_core != core)
            def _():
                wait(cb.at[pl.ds(0, 8)], z_send.at[f])

        wait(ga.at[f, 0, pl.ds(0, 3)], s1_send.at[f])
        wait(ga.at[f, 0, pl.ds(0, 12)], s2_send.at[f])
        wait(ga.at[f, 0], sib_send.at[f])

    def assemble(f):
        for cc in range(2):
            @pl.loop(0, 16)
            def _(s):
                p = s if cc == 0 else (s % 4) * 4 + s // 4
                for i in range(6):
                    k = 6 * cc + i
                    m = p * 3 + k // 4
                    chunk(x, m, (k % 4) * SLAB)[...] = ga[f, cc, s, i]

    def apply_terms():
        split(x, xh, xl, K, 64)

        @pl.loop(0, 3)
        def _(n):
            cols = pl.ds(pl.multiple_of(n * 256, 256), 256)
            uh[:, cols], ul[:, cols] = halves(product(lh[...], ll[...], xh, xl, cols))

        @pl.loop(0, 3)
        def _(n):
            cols = pl.ds(pl.multiple_of(n * 256, 256), 256)
            part[:, cols] = product(uh[...], ul[...], rh, rl, cols)

    @pl.when(is_owner)
    def _():
        mine[0] = chunk(a_ref, own)[...]

    gather_start(0)
    to_owners(l_ref, cb, c1_send, c1_recv)
    split(l_ref, lh, ll, SLAB, 48)
    split(r_ref, rh, rl, K, 64)
    gather_rest(0)

    ring_right, ring_left, ring_far = (r + 1) % 4, (r + 3) % 4, (r + 2) % 4

    def slab_half(rr, hh):
        return cf.at[pl.ds(pl.multiple_of(rr * SLAB + hh * 96, 96), 96)]

    for f in range(2):
        assemble(f)
        apply_terms()
        to_owners(part, rs.at[f], rs_send.at[f], rs_recv.at[f])
        if f == 0:
            @pl.when(is_owner)
            def _():
                wait(cb.at[pl.ds(0, 63)], c1_recv)

                @pl.loop(0, 64)
                def _(i):
                    j = (i + t) % 64
                    total = jnp.zeros((TR, TC), F32)
                    for c in range(FAN):
                        weight = jnp.where(c < count[j], wtable[windex[j, c]], 0.0)
                        total = total + weight * cb[(source[j, c] - t + 63) % 64]
                    co[j] = total
                    dst = chunk(cf, own, r * SLAB)

                    @pl.when(j != t)
                    def _():
                        remote(co.at[j], dst, c2_send, c2_recv, j, r).start()

                    @pl.when(j == t)
                    def _():
                        pltpu.make_async_copy(co.at[j], dst, c2_recv).start()
        else:
            wait(cf.at[pl.ds(pl.multiple_of(r * SLAB, SLAB), SLAB)], c2_recv)
            for hh, rr, sem in ((0, ring_right, 0), (1, ring_left, 2), (1, ring_right, 1), (0, ring_left, 3)):
                remote(slab_half(r, hh), slab_half(r, hh), c3_send, c3_recv.at[sem], t, rr).start()

        @pl.when(is_owner)
        def _():
            wait(rs.at[f, pl.ds(0, 63)], rs_recv.at[f])
            total = lax.fori_loop(0, 64, lambda i, s: s + rs[f, i], jnp.zeros((TR, TC), F32))
            mine[f + 1] = mine[f] - 0.3 * total

        to_owners_sent(rs_send.at[f])
        gather_start(f + 1)
        gather_rest(f + 1)

    assemble(2)
    squares = jnp.sum(lax.fori_loop(
        0, 96, lambda i, s: s + x[pl.ds(pl.multiple_of(i * 8, 8), 8), :] ** 2, jnp.zeros((8, K), F32)
    ))
    scale = 1.0 / jnp.sqrt(jnp.full((8, 128), squares, F32))[0:1, 0:1]

    @pl.loop(0, 12)
    def _(i):
        at = pl.ds(pl.multiple_of(i * 64, 64), 64)
        x[at, :] = x[at, :] * scale

    def transposed(src, high, low):
        @pl.loop(0, 3)
        def _(i):
            for n in range(3):
                at = pl.ds(pl.multiple_of(i * 256, 256), 256)
                to = pl.ds(n * 256, 256)
                high[to, at], low[to, at] = halves(src[at, to].T)

    for sweep in range(SWEEPS):
        split(x, xh, xl, K, 64)
        transposed(x, yh, yl)

        @pl.loop(0, 3)
        def _(n):
            cols = pl.ds(pl.multiple_of(n * 256, 256), 256)
            g[:, cols] = product(yh[...], yl[...], xh, xl, cols)

        split(g, yh, yl, K, 64)

        @pl.loop(0, 3)
        def _(n):
            cols = pl.ds(pl.multiple_of(n * 256, 256), 256)
            w[:, cols] = COEF_TWO * g[:, cols] + COEF_THREE * product(yh[...], yl[...], yh, yl, cols)

        split(w, yh, yl, K, 64)

        @pl.loop(0, 3)
        def _(n):
            cols = pl.ds(pl.multiple_of(n * 256, 256), 256)
            x[:, cols] = COEF_ONE * x[:, cols] + product(xh[...], xl[...], yh, yl, cols)

        if sweep == 0:
            wait(slab_half(ring_left, 0), c3_recv.at[0])
            remote(slab_half(ring_left, 0), slab_half(ring_left, 0), c3_send, c3_recv.at[4], t, ring_right).start()
            wait(slab_half(ring_right, 1), c3_recv.at[2])
            remote(slab_half(ring_right, 1), slab_half(ring_right, 1), c3_send, c3_recv.at[5], t, ring_left).start()

    @pl.loop(0, 12)
    def _(i):
        at = pl.ds(pl.multiple_of(i * 64, 64), 64)
        x[at, :] = x[at, :] * math.sqrt(K)

    my_rows = pl.ds(pl.multiple_of(r * SLAB, SLAB), SLAB)
    iso_ref[...] = x[my_rows, :]
    transposed(x, yh, yl)
    lh[...] = yh[my_rows, :]
    ll[...] = yl[my_rows, :]
    split(x, xh, xl, K, 64)
    for rr, hh, sem in ((ring_left, 1, 1), (ring_right, 0, 3), (ring_far, 0, 4), (ring_far, 1, 5)):
        wait(slab_half(rr, hh), c3_recv.at[sem])
    split(cf, rh, rl, K, 64)

    @pl.loop(0, 3)
    def _(n):
        cols = pl.ds(pl.multiple_of(n * 256, 256), 256)
        uh[:, cols], ul[:, cols] = halves(product(lh[...], ll[...], rh, rl, cols))

    @pl.loop(0, 3)
    def _(n):
        cols = pl.ds(pl.multiple_of(n * 256, 256), 256)
        env_ref[:, cols] = product(uh[...], ul[...], xh, xl, cols)

    for f in range(3):
        gather_sent(f)
    to_owners_sent(c1_send)

    @pl.when(is_owner)
    def _():
        wait(co.at[pl.ds(0, 63)], c2_send)

    wait(cf.at[pl.ds(0, 3 * SLAB)], c3_send)


def body(amplitudes, left_terms, right_terms, source_list, list_count, weight_index, weight_table):
    vmem = pl.BlockSpec(memory_space=pltpu.VMEM)
    smem = pl.BlockSpec(memory_space=pltpu.SMEM)
    dma = pltpu.SemaphoreType.DMA
    slab = jax.ShapeDtypeStruct((SLAB, K), F32)
    iso, env = pl.pallas_call(
        kernel,
        out_shape=(slab, slab),
        in_specs=[vmem] * 3 + [smem] * 4,
        out_specs=(vmem, vmem),
        scratch_shapes=[
            pltpu.VMEM((SLAB, K), BF), pltpu.VMEM((SLAB, K), BF),
            pltpu.VMEM((K, K), BF), pltpu.VMEM((K, K), BF),
            pltpu.VMEM((K, K), BF), pltpu.VMEM((K, K), BF),
            pltpu.VMEM((K, K), BF), pltpu.VMEM((K, K), BF),
            pltpu.VMEM((SLAB, K), BF), pltpu.VMEM((SLAB, K), BF),
            pltpu.VMEM((SLAB, K), F32),
            pltpu.VMEM((K, K), F32), pltpu.VMEM((K, K), F32), pltpu.VMEM((K, K), F32),
            pltpu.VMEM((3, 2, 16, 6, TR, TC), F32),
            pltpu.VMEM((2, 64, TR, TC), F32),
            pltpu.VMEM((3, TR, TC), F32),
            pltpu.VMEM((64, TR, TC), F32),
            pltpu.VMEM((64, TR, TC), F32),
            pltpu.VMEM((K, K), F32),
            dma((3,)), dma((3, 6)), dma((3,)), dma((3, 3)), dma((3,)), dma((3, 6)), dma((3,)), dma((3, 7)),
            dma((2,)), dma((2,)), dma, dma, dma, dma, dma, dma((6,)),
        ],
        compiler_params=pltpu.CompilerParams(
            collective_id=0, has_side_effects=True, vmem_limit_bytes=56 * 1024 * 1024
        ),
        cost_estimate=pl.CostEstimate(flops=28 * 10**9, bytes_accessed=8 * 10**6, transcendentals=0),
    )(
        amplitudes, left_terms.reshape(SLAB, K), right_terms.reshape(K, K),
        source_list, list_count, weight_index, weight_table,
    )
    return iso, env.reshape(1, SLAB, K)


def solution(mesh):
    placed = (P("rows", None), P("terms", "rows", None), P("terms", None, None), P(), P(), P(), P())
    return jax.shard_map(
        body,
        mesh=mesh,
        in_specs=placed,
        out_specs=(P("rows", None), P("terms", "rows", None)),
        check_vma=False,
    )
```

time: 1680 us -> 183 us (0.11)
  waiting for transfers between devices: 1540 us -> 0 us
  Pallas kernels: 0 us -> 175 us
  matrix products: 54.3 us -> 0 us
  blocking collectives: 40.7 us -> 0 us
    psum x2 -> x0, waiting for transfers between devices: 1020 us -> none  [apply_terms(): summed = lax.psum(partial_sum, 'terms')]
    all_gather x6 -> x0, waiting for transfers between devices: 285 us -> none  [the longest x3 168 us: gram_full(): gram_matrix = lax.all_gather(shared, 'rows', axis=1, tiled=True)]
    reduce_scatter x4 -> x0, waiting for transfers between devices: 207 us -> none  [the longest x3 159 us: gram_full(): lax.psum_scatter(gram_part, 'rows', scatter_dimension=1, tiled=True)]
    pallas_call x0 -> x1, Pallas kernels: none -> 175 us  [body(): pl.pallas_call(kernel, out_shape=(slab, slab), in_specs=[vmem] * 3 + [sme...]
    dot_general x17 -> x0, matrix products: 54.3 us -> none  [the longest x3 12.8 us: schulz_update(): jnp.dot(iterate, gram_matrix, precision=HIGH, preferred_element_type=jnp....]
    all_to_all x1 -> x0, blocking collectives: 30 us -> none  [body(): lax.all_to_all(combined, 'terms', split_axis=0, concat_axis=1, tiled=True)]
    all_to_all x1 -> x0, waiting for transfers between devices: 25.3 us -> none  [body(): lax.all_to_all(flat_blocks, 'terms', split_axis=1, concat_axis=0, tiled=T...]
  transfers between devices with their start and end apart: 13 -> 0, of which waited for: 12 -> 0; matrix products, arithmetic and copies ran while one was open for 0% -> 0% of each run, Pallas kernels for 0% -> 0%
where the time goes in v1:
time: 183 us; the launch traced here: 182 us
  Pallas kernels  175 us (96%)
  local copies, waits for them, and re-layouts  6.6 us (4%)
    pallas_call x1, Pallas kernels, body(): pl.pallas_call(kernel, out_shape=(slab, slab), in_specs=[vmem] * 3 + [sme...  175 us
    unnamed x4, local copies, waits for them, and re-layouts  6.6 us

profile of v1, /device:TPU:1, one launch (start us, length us, event | category | flops | bytes accessed | tf_op | source)
XLA Modules:
  0.0 182.5 jit_solution(14538277519427253410)
XLA Ops:
  0.6 1.4 copy.9.source
  2.0 1.4 copy.10.windex
  3.4 175.2 %shard_map.86 = (f32[192,768]{1,0:T(8,128)}, f32[192,768]{1,0:T(8,128)}) custom-call(f32[192,768]{1,0:T(8,128)} %a_ref.1, f32[192,768]{1,0:T(8,128)} %bitcast.5, f32[768,768]{1,0:T(8,128)} %bitcast.4, s32[64,4]{1,0:T(8,128)} %copy.9.source, s32[64]{0:T(128)} %count.1, s32[64,4]{1,0:T(8,128)} %copy.10.windex, f32[8]{0:T(128)} %wtable.1), custom_call_target="tpu_custom_call" | custom-call | flops 28000000000 | bytes 8000000 | tf_op jit(solution)/shard_map/pallas_call | solution.py:394
  178.7 1.9 %copy.13 = f32[192,768]{1,0:T(8,128)} copy(f32[192,768]{1,0:T(8,128)} %get-tuple-element.8) | data formatting | bytes 1179648
  180.6 1.9 %copy.14 = f32[1,192,768]{2,1,0:T(8,128)} copy(f32[1,192,768]{2,1,0:T(8,128)} %bitcast.3) | data formatting | bytes 1179648

commit v2 on v1

--- a/solution.py
+++ b/solution.py
@@ -48,10 +48,10 @@
 
 
 def kernel(
-    a_ref, l_ref, r_ref, source, count, windex, wtable,
+    a_ref, l_hbm, r_hbm, source, count, windex, wtable,
     iso_ref, env_ref,
     lh, ll, rh, rl, xh, xl, yh, yl, uh, ul, part, x, g, w,
-    ga, rs, mine, cb, co, cf,
+    ga, rs, mine, cb, co, cf, l_ref, in_sem,
     z_send, z_recv, s1_send, s1_recv, s2_send, s2_recv, sib_send, sib_recv,
     rs_send, rs_recv, c1_send, c1_recv, c2_send, c2_recv, c3_send, c3_recv,
 ):
@@ -89,6 +89,10 @@
             device_id=there(tt, rr), device_id_type=MESH,
         )
 
+    bring_l = pltpu.make_async_copy(l_hbm, l_ref, in_sem.at[0])
+    bring_r = pltpu.make_async_copy(r_hbm, w, in_sem.at[1])
+    bring_l.start()
+    bring_r.start()
     barrier = pltpu.get_barrier_semaphore()
 
     @pl.loop(1, 64)
@@ -101,12 +105,16 @@
                 pl.semaphore_signal(
                     barrier, inc=1, device_id=there(term(cx, zz, cy, cc), (r + dr) % 4), device_id_type=MESH
                 )
+    bring_l.wait()
+    split(l_ref, lh, ll, SLAB, 48)
+    bring_r.wait()
+    split(w, rh, rl, K, 64)
     pl.semaphore_wait(barrier, 75)
 
-    def to_owners(src, dst, send, recv):
-        @pl.loop(0, OWNERS)
+    def to_owners(src, dst, send, recv, side):
+        @pl.loop(0, OWNERS // 2)
         def _(i):
-            m = (i + own) % OWNERS
+            m = 2 * ((i + own // 2) % (OWNERS // 2)) + side
             o = owner_term(m)
             slot = (t - o + 63) % 64
 
@@ -114,9 +122,10 @@
             def _():
                 remote(chunk(src, m), dst.at[slot], send, recv, o, r).start()
 
-        @pl.when(is_owner)
-        def _():
-            dst[63] = chunk(src, own)[...]
+        if side == 1:
+            @pl.when(is_owner)
+            def _():
+                dst[63] = chunk(src, own)[...]
 
     def to_owners_sent(send):
         @pl.when(is_owner)
@@ -140,9 +149,6 @@
         return term(jnp.where(core == 0, bb, aa), zl, jnp.where(core == 0, aa, bb), core)
 
     sibling = term(cx, zl, cy, 1 - core)
-
-    def half(f, cc, bb, hh):
-        return ga.at[f, cc, pl.ds(bb * 4 + 2 * hh, 2)]
 
     def gather_start(f):
         @pl.when(is_owner)
@@ -165,48 +171,42 @@
     def gather_rest(f):
         for i in range(6):
             wait(ga.at[f, core, here, i], z_recv.at[f, i])
-        block = ga.at[f, core, here]
-        for d in range(1, 4):
-            remote(block, block, s1_send.at[f], s1_recv.at[f, d - 1], partner(side_b, (side_a + d) % 4), r).start()
-        for d in range(1, 4):
-            wait(ga.at[f, core, side_b * 4 + (side_a + 4 - d) % 4], s1_recv.at[f, d - 1])
-
-        def push(src, tt, sem):
-            remote(src, src, s2_send.at[f], s2_recv.at[f, sem], tt, r).start()
-
-        def across(src, sem):
-            remote(src, src, sib_send.at[f], sib_recv.at[f, sem], sibling, r).start()
+
+        def block(bb, d):
+            return ga.at[f, core, bb * 4 + (side_a + 4 - d) % 4]
+
+        def across(bb, d, sem):
+            remote(block(bb, d), block(bb, d), sib_send.at[f], sib_recv.at[f, sem], sibling, r).start()
+
+        def push(bb, d, tt, sem):
+            remote(block(bb, d), block(bb, d), s2_send.at[f], s2_recv.at[f, sem], tt, r).start()
 
         to_right, to_left = partner(right, side_a), partner(left, side_a)
-        push(half(f, core, side_b, 0), to_right, 0)
-        push(half(f, core, side_b, 1), to_left, 2)
-        push(half(f, core, side_b, 1), to_right, 1)
-        push(half(f, core, side_b, 0), to_left, 3)
-        across(ga.at[f, core, pl.ds(side_b * 4, 4)], 0)
-        wait(half(f, core, left, 0), s2_recv.at[f, 0])
-        push(half(f, core, left, 0), to_right, 4)
-        wait(half(f, core, right, 1), s2_recv.at[f, 2])
-        push(half(f, core, right, 1), to_left, 5)
-        across(half(f, core, left, 0), 1)
-        across(half(f, core, right, 1), 2)
-        wait(half(f, core, left, 1), s2_recv.at[f, 1])
-        across(half(f, core, left, 1), 3)
-        wait(half(f, core, right, 0), s2_recv.at[f, 3])
-        across(half(f, core, right, 0), 4)
-        wait(half(f, core, opposite, 0), s2_recv.at[f, 4])
-        across(half(f, core, opposite, 0), 5)
-        wait(half(f, core, opposite, 1), s2_recv.at[f, 5])
-        across(half(f, core, opposite, 1), 6)
-        sb = side_a
-        sr, sl, so = (sb + 1) % 4, (sb + 3) % 4, (sb + 2) % 4
-        oc = 1 - core
-        wait(ga.at[f, oc, pl.ds(sb * 4, 4)], sib_recv.at[f, 0])
-        wait(half(f, oc, sl, 0), sib_recv.at[f, 1])
-        wait(half(f, oc, sr, 1), sib_recv.at[f, 2])
-        wait(half(f, oc, sl, 1), sib_recv.at[f, 3])
-        wait(half(f, oc, sr, 0), sib_recv.at[f, 4])
-        wait(half(f, oc, so, 0), sib_recv.at[f, 5])
-        wait(half(f, oc, so, 1), sib_recv.at[f, 6])
+        mine_now = block(side_b, 0)
+        for d in (1, 3, 2):
+            remote(mine_now, mine_now, s1_send.at[f], s1_recv.at[f, d - 1], partner(side_b, (side_a + d) % 4), r).start()
+        order = (0, 1, 3, 2)
+        for d in order:
+            if d > 0:
+                wait(block(side_b, d), s1_recv.at[f, d - 1])
+            push(side_b, d, to_right, d)
+            push(side_b, d, to_left, 4 + d)
+            across(side_b, d, d)
+        for d in order:
+            wait(block(left, d), s2_recv.at[f, d])
+            if d in (0, 3):
+                push(left, d, to_right, 8 + d)
+            wait(block(right, d), s2_recv.at[f, 4 + d])
+            if d in (1, 2):
+                push(right, d, to_left, 8 + d)
+            across(left, d, 4 + d)
+            across(right, d, 8 + d)
+        for d in order:
+            wait(block(opposite, d), s2_recv.at[f, 8 + d])
+            across(opposite, d, 12 + d)
+        for n, bb in enumerate((side_a, (side_a + 3) % 4, (side_a + 1) % 4, (side_a + 2) % 4)):
+            for d in order:
+                wait(ga.at[f, 1 - core, bb * 4 + (side_b + 4 - d) % 4], sib_recv.at[f, 4 * n + d])
 
     def gather_sent(f):
         @pl.when(is_owner)
@@ -233,7 +233,7 @@
                     m = p * 3 + k // 4
                     chunk(x, m, (k % 4) * SLAB)[...] = ga[f, cc, s, i]
 
-    def apply_terms():
+    def apply_terms(f):
         split(x, xh, xl, K, 64)
 
         @pl.loop(0, 3)
@@ -241,19 +241,21 @@
             cols = pl.ds(pl.multiple_of(n * 256, 256), 256)
             uh[:, cols], ul[:, cols] = halves(product(lh[...], ll[...], xh, xl, cols))
 
-        @pl.loop(0, 3)
-        def _(n):
-            cols = pl.ds(pl.multiple_of(n * 256, 256), 256)
-            part[:, cols] = product(uh[...], ul[...], rh, rl, cols)
+        for side, tiles in ((0, 2), (1, 1)):
+            @pl.loop(0, tiles)
+            def _(n):
+                cols = pl.ds(pl.multiple_of((n + 2 * side) * 256, 256), 256)
+                part[:, cols] = product(uh[...], ul[...], rh, rl, cols)
+
+            to_owners(part, rs.at[f], rs_send.at[f], rs_recv.at[f], side)
 
     @pl.when(is_owner)
     def _():
         mine[0] = chunk(a_ref, own)[...]
 
     gather_start(0)
-    to_owners(l_ref, cb, c1_send, c1_recv)
-    split(l_ref, lh, ll, SLAB, 48)
-    split(r_ref, rh, rl, K, 64)
+    to_owners(l_ref, cb, c1_send, c1_recv, 0)
+    to_owners(l_ref, cb, c1_send, c1_recv, 1)
     gather_rest(0)
 
     ring_right, ring_left, ring_far = (r + 1) % 4, (r + 3) % 4, (r + 2) % 4
@@ -263,8 +265,7 @@
 
     for f in range(2):
         assemble(f)
-        apply_terms()
-        to_owners(part, rs.at[f], rs_send.at[f], rs_recv.at[f])
+        apply_terms(f)
         if f == 0:
             @pl.when(is_owner)
             def _():
@@ -275,8 +276,8 @@
                     j = (i + t) % 64
                     total = jnp.zeros((TR, TC), F32)
                     for c in range(FAN):
-                        weight = jnp.where(c < count[j], wtable[windex[j, c]], 0.0)
-                        total = total + weight * cb[(source[j, c] - t + 63) % 64]
+                        weight = jnp.where(c < count[j], wtable[windex[c, j]], 0.0)
+                        total = total + weight * cb[(source[c, j] - t + 63) % 64]
                     co[j] = total
                     dst = chunk(cf, own, r * SLAB)
 
@@ -288,9 +289,10 @@
                     def _():
                         pltpu.make_async_copy(co.at[j], dst, c2_recv).start()
         else:
-            wait(cf.at[pl.ds(pl.multiple_of(r * SLAB, SLAB), SLAB)], c2_recv)
-            for hh, rr, sem in ((0, ring_right, 0), (1, ring_left, 2), (1, ring_right, 1), (0, ring_left, 3)):
-                remote(slab_half(r, hh), slab_half(r, hh), c3_send, c3_recv.at[sem], t, rr).start()
+            wait(slab_half(ring_left, 0), c3_recv.at[0])
+            remote(slab_half(ring_left, 0), slab_half(ring_left, 0), c3_send, c3_recv.at[4], t, ring_right).start()
+            wait(slab_half(ring_right, 1), c3_recv.at[2])
+            remote(slab_half(ring_right, 1), slab_half(ring_right, 1), c3_send, c3_recv.at[5], t, ring_left).start()
 
         @pl.when(is_owner)
         def _():
@@ -300,6 +302,10 @@
 
         to_owners_sent(rs_send.at[f])
         gather_start(f + 1)
+        if f == 0:
+            wait(cf.at[pl.ds(pl.multiple_of(r * SLAB, SLAB), SLAB)], c2_recv)
+            for hh, rr, sem in ((0, ring_right, 0), (1, ring_left, 2), (1, ring_right, 1), (0, ring_left, 3)):
+                remote(slab_half(r, hh), slab_half(r, hh), c3_send, c3_recv.at[sem], t, rr).start()
         gather_rest(f + 1)
 
     assemble(2)
@@ -343,12 +349,6 @@
         def _(n):
             cols = pl.ds(pl.multiple_of(n * 256, 256), 256)
             x[:, cols] = COEF_ONE * x[:, cols] + product(xh[...], xl[...], yh, yl, cols)
-
-        if sweep == 0:
-            wait(slab_half(ring_left, 0), c3_recv.at[0])
-            remote(slab_half(ring_left, 0), slab_half(ring_left, 0), c3_send, c3_recv.at[4], t, ring_right).start()
-            wait(slab_half(ring_right, 1), c3_recv.at[2])
-            remote(slab_half(ring_right, 1), slab_half(ring_right, 1), c3_send, c3_recv.at[5], t, ring_left).start()
 
     @pl.loop(0, 12)
     def _(i):
@@ -394,7 +394,7 @@
     iso, env = pl.pallas_call(
         kernel,
         out_shape=(slab, slab),
-        in_specs=[vmem] * 3 + [smem] * 4,
+        in_specs=[vmem] + [pl.BlockSpec(memory_space=pl.ANY)] * 2 + [smem] * 4,
         out_specs=(vmem, vmem),
         scratch_shapes=[
             pltpu.VMEM((SLAB, K), BF), pltpu.VMEM((SLAB, K), BF),
@@ -410,7 +410,9 @@
             pltpu.VMEM((64, TR, TC), F32),
             pltpu.VMEM((64, TR, TC), F32),
             pltpu.VMEM((K, K), F32),
-            dma((3,)), dma((3, 6)), dma((3,)), dma((3, 3)), dma((3,)), dma((3, 6)), dma((3,)), dma((3, 7)),
+            pltpu.VMEM((SLAB, K), F32),
+            dma((2,)),
+            dma((3,)), dma((3, 6)), dma((3,)), dma((3, 3)), dma((3,)), dma((3, 12)), dma((3,)), dma((3, 16)),
             dma((2,)), dma((2,)), dma, dma, dma, dma, dma, dma((6,)),
         ],
         compiler_params=pltpu.CompilerParams(
@@ -419,7 +421,7 @@
         cost_estimate=pl.CostEstimate(flops=28 * 10**9, bytes_accessed=8 * 10**6, transcendentals=0),
     )(
         amplitudes, left_terms.reshape(SLAB, K), right_terms.reshape(K, K),
-        source_list, list_count, weight_index, weight_table,
+        source_list.T, list_count, weight_index.T, weight_table,
     )
     return iso, env.reshape(1, SLAB, K)
 

time: 183 us -> 172 us (0.940)
  Pallas kernels: 175 us -> 167 us
  local copies, waits for them, and re-layouts: 6.6 us -> 3.83 us
    pallas_call x1, Pallas kernels: 175 us -> 167 us  [body(): pl.pallas_call(kernel, out_shape=(slab, slab), in_specs=[vmem] + [pl.Bloc...]
    unnamed x4 -> x2, local copies, waits for them, and re-layouts: 6.6 us -> 3.83 us
where the time goes in v2:
time: 172 us
  Pallas kernels  167 us (97%)
  local copies, waits for them, and re-layouts  3.83 us (2%)
    pallas_call x1, Pallas kernels, body(): pl.pallas_call(kernel, out_shape=(slab, slab), in_specs=[vmem] + [pl.Bloc...  167 us
    unnamed x2, local copies, waits for them, and re-layouts  3.83 us

profile of v2, /device:TPU:1, one launch (start us, length us, event | category | flops | bytes accessed | tf_op | source)
XLA Modules:
  0.0 171.8 jit_solution(969381283064141818)
XLA Ops:
  0.6 167.4 %shard_map.86 = (f32[192,768]{1,0:T(8,128)}, f32[192,768]{1,0:T(8,128)}) custom-call(f32[192,768]{1,0:T(8,128)} %a_ref.1, f32[192,768]{1,0:T(8,128)} %bitcast.7, f32[768,768]{1,0:T(8,128)} %bitcast.6, s32[4,64]{1,0:T(4,128)} %bitcast.8, s32[64]{0:T(128)} %count.1, s32[4,64]{1,0:T(4,128)} %bitcast.9, f32[8]{0:T(128)} %wtable.1), custom_call_target="tpu_custom_call" | custom-call | flops 28000000000 | bytes 8000000 | tf_op jit(solution)/shard_map/pallas_call | solution.py:394
  168.0 1.9 %copy.11 = f32[192,768]{1,0:T(8,128)} copy(f32[192,768]{1,0:T(8,128)} %get-tuple-element.8) | data formatting | bytes 1179648
  169.9 1.9 %copy.12 = f32[1,192,768]{2,1,0:T(8,128)} copy(f32[1,192,768]{2,1,0:T(8,128)} %bitcast.5) | data formatting | bytes 1179648

commit v3 on v2

v3 whole, which is shorter than its diff:
```python
import math

import jax
import jax.numpy as jnp
from jax import lax
from jax.experimental import pallas as pl
from jax.experimental.pallas import tpu as pltpu
from jax.sharding import PartitionSpec as P

K = 768
FAN = 4
SWEEPS = 3
SLAB = 192
OWNERS = 48
TR, TC = 8, 384
COEF_ONE = 3.4445
COEF_TWO = -4.775
COEF_THREE = 2.0315
MESH = pl.DeviceIdType.MESH
BF = jnp.bfloat16
F32 = jnp.float32


def halves(value):
    high = value.astype(BF)
    return high, (value - high.astype(F32)).astype(BF)


def split(src, high, low, rows, step):
    @pl.loop(0, rows // step)
    def _(i):
        at = pl.ds(pl.multiple_of(i * step, step), step)
        high[at, :], low[at, :] = halves(src[at, :])


def product(ah, al, bh, bl, cols):
    left_h, left_l = ah, al
    rh, rl = bh[:, cols], bl[:, cols]
    return jnp.dot(
        jnp.concatenate([left_h, left_h, left_l], axis=1),
        jnp.concatenate([rh, rl, rh], axis=0),
        preferred_element_type=F32,
    )


def wait(ref, sem):
    pltpu.make_async_copy(ref, ref, sem).wait()


def kernel(
    a_ref, l_hbm, r_hbm, source, count, windex, wtable,
    iso_ref, env_ref,
    lh, ll, rh, rl, xh, xl, vh, vl, yh, yl, gh, gl, wh, wl, uh, ul, part, x, w, pre,
    ga, rs, mine, cb, co, cf, l_ref, in_sem,
    z_send, z_recv, s1_send, s1_recv, s2_send, s2_recv, sib_send, sib_recv,
    pre_send, pre_recv, rs_send, rs_recv, c1_send, c1_recv, c2_send, c2_recv, c3_send, c3_recv,
):
    t = lax.axis_index("terms")
    r = lax.axis_index("rows")
    core = t % 2
    cy = (t // 2) % 4
    zl = (t // 8) % 2
    cx = t // 16
    pos = cx * 4 + cy
    dq = zl * 2 + core
    q = jnp.where(pos % 2 == 1, 3 - dq, dq)
    is_owner = q < 3
    own = jnp.minimum(pos * 3 + q, OWNERS - 1)

    def term(xx, zz, yy, cc):
        return ((xx * 2 + zz) * 4 + yy) * 2 + cc

    def owner_term(m):
        p = m // 3
        qq = m % 3
        d = jnp.where(p % 2 == 1, 3 - qq, qq)
        return term(p // 4, d // 2, p % 4, d % 2)

    def chunk(ref, m, row0=0):
        rows = pl.ds(pl.multiple_of(row0 + (m // 2) * TR, TR), TR)
        return ref.at[rows, pl.ds(pl.multiple_of((m % 2) * TC, TC), TC)]

    def there(tt, rr):
        return {"terms": tt, "rows": rr}

    def remote(src, dst, send, recv, tt, rr):
        return pltpu.make_async_remote_copy(
            src_ref=src, dst_ref=dst, send_sem=send, recv_sem=recv,
            device_id=there(tt, rr), device_id_type=MESH,
        )

    bring_l = pltpu.make_async_copy(l_hbm, l_ref, in_sem.at[0])
    bring_r = pltpu.make_async_copy(r_hbm, w, in_sem.at[1])
    bring_l.start()
    bring_r.start()
    barrier = pltpu.get_barrier_semaphore()

    @pl.loop(1, 64)
    def _(i):
        pl.semaphore_signal(barrier, inc=1, device_id=there((t + i) % 64, r), device_id_type=MESH)

    for dr in range(1, 4):
        for zz in range(2):
            for cc in range(2):
                pl.semaphore_signal(
                    barrier, inc=1, device_id=there(term(cx, zz, cy, cc), (r + dr) % 4), device_id_type=MESH
                )
    bring_l.wait()
    split(l_ref, lh, ll, SLAB, 48)
    bring_r.wait()
    split(w, rh, rl, K, 64)
    pl.semaphore_wait(barrier, 75)

    def to_owners(src, dst, send, recv):
        @pl.loop(0, OWNERS)
        def _(i):
            m = (i + own) % OWNERS
            o = owner_term(m)
            slot = (t - o + 63) % 64

            @pl.when(o != t)
            def _():
                remote(chunk(src, m), dst.at[slot], send, recv, o, r).start()

        @pl.when(is_owner)
        def _():
            dst[63] = chunk(src, own)[...]

    def to_owners_sent(send):
        @pl.when(is_owner)
        def _():
            wait(cb.at[pl.ds(0, 47)], send)

        @pl.when(jnp.logical_not(is_owner))
        def _():
            wait(cb.at[pl.ds(0, 48)], send)

    sibling = term(cx, zl, cy, 1 - core)
    kept = pl.ds(pl.multiple_of(core * 96, 96), 96)
    given = pl.ds(pl.multiple_of((1 - core) * 96, 96), 96)
    keeps_own = jnp.logical_and(is_owner, own // 24 == core)

    def tile(n):
        return pl.ds(n * 256, 256)

    def pre_start(f, n):
        remote(part.at[given, tile(n)], pre.at[f, :, tile(n)], pre_send.at[f], pre_recv.at[f, n], sibling, r).start()

    def pre_add(f, n):
        wait(pre.at[f, :, tile(n)], pre_recv.at[f, n])
        part[kept, tile(n)] = part[kept, tile(n)] + pre[f, :, tile(n)]

    def reduce_start(f, side):
        @pl.loop(0, 12)
        def _(i):
            m = 24 * core + 2 * ((i + pos) % 12) + side
            o = owner_term(m)
            dst = rs.at[f, (t // 2 - o // 2 + 31) % 32]

            @pl.when(o != t)
            def _():
                remote(chunk(part, m), dst, rs_send.at[f], rs_recv.at[f], o, r).start()

            @pl.when(o == t)
            def _():
                pltpu.make_async_copy(chunk(part, m), dst, rs_recv.at[f]).start()

    def reduce_sent(f):
        wait(pre.at[f], pre_send.at[f])

        @pl.when(keeps_own)
        def _():
            wait(rs.at[f, pl.ds(0, 23)], rs_send.at[f])

        @pl.when(jnp.logical_not(keeps_own))
        def _():
            wait(rs.at[f, pl.ds(0, 24)], rs_send.at[f])

    side_b = jnp.where(core == 0, cx, cy)
    side_a = jnp.where(core == 0, cy, cx)
    here = side_b * 4 + side_a
    kk = 4 * jnp.minimum(q, 2) + r
    to_core = kk // 6
    to_slot = kk % 6
    to_pos = jnp.where(to_core == 0, cx * 4 + cy, cy * 4 + cx)

    def partner(bb, aa):
        return term(jnp.where(core == 0, bb, aa), zl, jnp.where(core == 0, aa, bb), core)

    def gather_start(f):
        @pl.when(is_owner)
        def _():
            for dz in range(2):
                for dr in range(4):
                    tt, rr = term(cx, (zl + dz) % 2, cy, to_core), (r + dr) % 4
                    dst = ga.at[f, to_core, to_pos, to_slot]
                    if dz == 0 and dr == 0:
                        @pl.when(to_core == core)
                        def _():
                            pltpu.make_async_copy(mine.at[f], dst, z_recv.at[f, to_slot]).start()

                        @pl.when(to_core != core)
                        def _():
                            remote(mine.at[f], dst, z_send.at[f], z_recv.at[f, to_slot], tt, rr).start()
                    else:
                        remote(mine.at[f], dst, z_send.at[f], z_recv.at[f, to_slot], tt, rr).start()

    def gather_rest(f, after_z=None, after_push=None):
        for i in range(6):
            wait(ga.at[f, core, here, i], z_recv.at[f, i])

        def block(bb, d):
            return ga.at[f, core, bb * 4 + (side_a + 4 - d) % 4]

        def across(bb, d, sem):
            remote(block(bb, d), block(bb, d), sib_send.at[f], sib_recv.at[f, sem], sibling, r).start()

        def push(bb, d, tt, sem):
            remote(block(bb, d), block(bb, d), s2_send.at[f], s2_recv.at[f, sem], tt, r).start()

        mine_now = block(side_b, 0)
        for d in (1, 3, 2):
            remote(mine_now, mine_now, s1_send.at[f], s1_recv.at[f, d - 1], partner(side_b, (side_a + d) % 4), r).start()
        if after_z:
            after_z()
        order = (0, 1, 3, 2)
        for d in order:
            if d > 0:
                wait(block(side_b, d), s1_recv.at[f, d - 1])
            for n in (1, 3, 2):
                push(side_b, d, partner((side_b + n) % 4, side_a), 4 * (n - 1) + d)
            across(side_b, d, d)
        if after_push:
            after_push()
        for n in (1, 3, 2):
            for d in order:
                bb = (side_b + 4 - n) % 4
                wait(block(bb, d), s2_recv.at[f, 4 * (n - 1) + d])
                across(bb, d, 4 * n + d)
        for n in (0, 1, 3, 2):
            for d in order:
                bb = (side_a + 4 - n) % 4
                wait(ga.at[f, 1 - core, bb * 4 + (side_b + 4 - d) % 4], sib_recv.at[f, 4 * n + d])

    def gather_sent(f):
        @pl.when(is_owner)
        def _():
            @pl.when(to_core == core)
            def _():
                wait(cb.at[pl.ds(0, 7)], z_send.at[f])

            @pl.when(to_core != core)
            def _():
                wait(cb.at[pl.ds(0, 8)], z_send.at[f])

        wait(ga.at[f, 0, pl.ds(0, 3)], s1_send.at[f])
        wait(ga.at[f, 0, pl.ds(0, 12)], s2_send.at[f])
        wait(ga.at[f, 0], sib_send.at[f])

    def assemble(f):
        for cc in range(2):
            @pl.loop(0, 16)
            def _(s):
                p = s if cc == 0 else (s % 4) * 4 + s // 4
                for i in range(6):
                    k = 6 * cc + i
                    m = p * 3 + k // 4
                    chunk(x, m, (k % 4) * SLAB)[...] = ga[f, cc, s, i]

    def apply_terms(f):
        split(x, xh, xl, K, 64)

        @pl.loop(0, 3)
        def _(n):
            cols = pl.ds(pl.multiple_of(n * 256, 256), 256)
            uh[:, cols], ul[:, cols] = halves(product(lh[...], ll[...], xh, xl, cols))

        for n in range(3):
            part[:, tile(n)] = product(uh[...], ul[...], rh, rl, tile(n))
            pre_start(f, n)
        pre_add(f, 0)
        pre_add(f, 1)
        reduce_start(f, 0)
        pre_add(f, 2)
        reduce_start(f, 1)

    @pl.when(is_owner)
    def _():
        mine[0] = chunk(a_ref, own)[...]

    gather_start(0)
    to_owners(l_ref, cb, c1_send, c1_recv)
    gather_rest(0)

    ring_right, ring_left, ring_far = (r + 1) % 4, (r + 3) % 4, (r + 2) % 4

    def slab_half(rr, hh):
        return cf.at[pl.ds(pl.multiple_of(rr * SLAB + hh * 96, 96), 96)]

    def go_round(rr, hh, to, sem):
        remote(slab_half(rr, hh), slab_half(rr, hh), c3_send, c3_recv.at[sem], t, to).start()

    def mix():
        @pl.when(is_owner)
        def _():
            wait(cb.at[pl.ds(0, 63)], c1_recv)

            @pl.loop(0, 64)
            def _(j):
                total = jnp.zeros((TR, TC), F32)
                for c in range(FAN):
                    weight = jnp.where(c < count[j], wtable[windex[c, j]], 0.0)
                    total = total + weight * cb[(source[c, j] - t + 63) % 64]
                co[j] = total

    def give_back():
        @pl.when(is_owner)
        def _():
            dst = chunk(cf, own, r * SLAB)

            @pl.loop(1, 64)
            def _(i):
                j = (i + t) % 64
                remote(co.at[j], dst, c2_send, c2_recv, j, r).start()

            pltpu.make_async_copy(co.at[t], dst, c2_recv).start()

    def first_round():
        wait(cf.at[pl.ds(pl.multiple_of(r * SLAB, SLAB), SLAB)], c2_recv)
        go_round(r, 0, ring_right, 0)
        go_round(r, 1, ring_left, 2)

    def second_round():
        go_round(r, 1, ring_right, 1)
        go_round(r, 0, ring_left, 3)
        wait(slab_half(ring_left, 0), c3_recv.at[0])
        go_round(ring_left, 0, ring_right, 4)
        wait(slab_half(ring_right, 1), c3_recv.at[2])
        go_round(ring_right, 1, ring_left, 5)

    for f in range(2):
        assemble(f)
        apply_terms(f)
        if f == 0:
            mix()

        @pl.when(is_owner)
        def _():
            wait(rs.at[f], rs_recv.at[f])
            mine[f + 1] = mine[f] - 0.3 * jnp.sum(rs[f], axis=0)

        gather_start(f + 1)
        if f == 0:
            give_back()
        reduce_sent(f)
        if f == 0:
            gather_rest(1, after_push=first_round)
        else:
            gather_rest(2, after_z=second_round)

    assemble(2)
    squares = jnp.sum(lax.fori_loop(
        0, 12,
        lambda i, s: s + jnp.sum((x[pl.ds(pl.multiple_of(i * 64, 64), 64), :] ** 2).reshape(8, 8, K), axis=0),
        jnp.zeros((8, K), F32),
    ))
    scale = 1.0 / jnp.sqrt(jnp.full((8, 128), squares, F32))[0:1, 0:1]
    for n in range(3):
        value = x[tile(n), :] * scale
        xh[tile(n), :], xl[tile(n), :] = halves(value)
        yh[:, tile(n)], yl[:, tile(n)] = halves(value.T)

    def symmetric(ah, al, bh, bl, oh, ol, last):
        for n in range(3):
            top = 256 * (n + 1)
            value = last(product(ah[:top, :], al[:top, :], bh, bl, tile(n)), n)
            oh[:top, tile(n)], ol[:top, tile(n)] = halves(value)
            for m in range(n):
                oh[tile(n), tile(m)], ol[tile(n), tile(m)] = halves(value[256 * m:256 * (m + 1)].T)

    def polynomial(value, n):
        top = value.shape[0]
        gram = gh[:top, tile(n)].astype(F32) + gl[:top, tile(n)].astype(F32)
        row = lax.broadcasted_iota(jnp.int32, value.shape, 0)
        col = lax.broadcasted_iota(jnp.int32, value.shape, 1) + 256 * n
        return COEF_TWO * gram + COEF_THREE * value + jnp.where(row == col, COEF_ONE, 0.0)

    now, later = (xh, xl), (vh, vl)
    for sweep in range(SWEEPS):
        symmetric(yh, yl, now[0], now[1], gh, gl, lambda value, n: value)
        symmetric(gh, gl, gh, gl, wh, wl, polynomial)
        for n in range(3):
            value = product(now[0][...], now[1][...], wh, wl, tile(n))
            if sweep == SWEEPS - 1:
                value = value * math.sqrt(K)
                x[:, tile(n)] = value
            later[0][:, tile(n)], later[1][:, tile(n)] = halves(value)
            yh[tile(n), :], yl[tile(n), :] = halves(value.T)
        now, later = later, now

    my_rows = pl.ds(pl.multiple_of(r * SLAB, SLAB), SLAB)
    iso_ref[...] = x[my_rows, :]
    for rr, hh, sem in ((ring_left, 1, 1), (ring_right, 0, 3), (ring_far, 0, 4), (ring_far, 1, 5)):
        wait(slab_half(rr, hh), c3_recv.at[sem])
    split(cf, gh, gl, K, 64)

    for n in range(3):
        uh[:, tile(n)], ul[:, tile(n)] = halves(product(yh[my_rows, :], yl[my_rows, :], gh, gl, tile(n)))
    for n in range(3):
        env_ref[:, tile(n)] = product(uh[...], ul[...], now[0], now[1], tile(n))

    for f in range(3):
        gather_sent(f)
    to_owners_sent(c1_send)

    @pl.when(is_owner)
    def _():
        wait(co.at[pl.ds(0, 63)], c2_send)

    wait(cf.at[pl.ds(0, 3 * SLAB)], c3_send)


def body(amplitudes, left_terms, right_terms, source_list, list_count, weight_index, weight_table):
    vmem = pl.BlockSpec(memory_space=pltpu.VMEM)
    smem = pl.BlockSpec(memory_space=pltpu.SMEM)
    dma = pltpu.SemaphoreType.DMA
    slab = jax.ShapeDtypeStruct((SLAB, K), F32)
    iso, env = pl.pallas_call(
        kernel,
        out_shape=(slab, slab),
        in_specs=[vmem] + [pl.BlockSpec(memory_space=pl.ANY)] * 2 + [smem] * 4,
        out_specs=(vmem, vmem),
        scratch_shapes=[
            pltpu.VMEM((SLAB, K), BF), pltpu.VMEM((SLAB, K), BF),
            *[pltpu.VMEM((K, K), BF)] * 12,
            pltpu.VMEM((SLAB, K), BF), pltpu.VMEM((SLAB, K), BF),
            pltpu.VMEM((SLAB, K), F32),
            pltpu.VMEM((K, K), F32), pltpu.VMEM((K, K), F32), pltpu.VMEM((2, 96, K), F32),
            pltpu.VMEM((3, 2, 16, 6, TR, TC), F32),
            pltpu.VMEM((2, 32, TR, TC), F32),
            pltpu.VMEM((3, TR, TC), F32),
            pltpu.VMEM((64, TR, TC), F32),
            pltpu.VMEM((64, TR, TC), F32),
            pltpu.VMEM((K, K), F32),
            pltpu.VMEM((SLAB, K), F32),
            dma((2,)),
            dma((3,)), dma((3, 6)), dma((3,)), dma((3, 3)), dma((3,)), dma((3, 12)), dma((3,)), dma((3, 16)),
            dma((2,)), dma((2, 3)), dma((2,)), dma((2,)), dma, dma, dma, dma, dma, dma((6,)),
        ],
        compiler_params=pltpu.CompilerParams(
            collective_id=0, has_side_effects=True, vmem_limit_bytes=56 * 1024 * 1024
        ),
        cost_estimate=pl.CostEstimate(flops=28 * 10**9, bytes_accessed=8 * 10**6, transcendentals=0),
    )(
        amplitudes, left_terms.reshape(SLAB, K), right_terms.reshape(K, K),
        source_list.T, list_count, weight_index.T, weight_table,
    )
    return iso, env.reshape(1, SLAB, K)


def solution(mesh):
    placed = (P("rows", None), P("terms", "rows", None), P("terms", None, None), P(), P(), P(), P())
    return jax.shard_map(
        body,
        mesh=mesh,
        in_specs=placed,
        out_specs=(P("rows", None), P("terms", "rows", None)),
        check_vma=False,
    )
```

time: 172 us -> 137 us (0.80)
  Pallas kernels: 167 us -> 132 us
    pallas_call x1, Pallas kernels: 167 us -> 132 us  [body(): pl.pallas_call(kernel, out_shape=(slab, slab), in_specs=[vmem] + [pl.Bloc...]
where the time goes in v3:
time: 137 us
  Pallas kernels  132 us (96%)
  local copies, waits for them, and re-layouts  3.83 us (3%)
    pallas_call x1, Pallas kernels, body(): pl.pallas_call(kernel, out_shape=(slab, slab), in_specs=[vmem] + [pl.Bloc...  132 us
    unnamed x2, local copies, waits for them, and re-layouts  3.83 us

profile of v3, /device:TPU:1, one launch (start us, length us, event | category | flops | bytes accessed | tf_op | source)
XLA Modules:
  0.0 136.6 jit_solution(13111220505175983840)
XLA Ops:
  0.6 132.2 %shard_map.86 = (f32[192,768]{1,0:T(8,128)}, f32[192,768]{1,0:T(8,128)}) custom-call(f32[192,768]{1,0:T(8,128)} %a_ref.1, f32[192,768]{1,0:T(8,128)} %bitcast.7, f32[768,768]{1,0:T(8,128)} %bitcast.6, s32[4,64]{1,0:T(4,128)} %bitcast.8, s32[64]{0:T(128)} %count.1, s32[4,64]{1,0:T(4,128)} %bitcast.9, f32[8]{0:T(128)} %wtable.1), custom_call_target="tpu_custom_call" | custom-call | flops 28000000000 | bytes 8000000 | tf_op jit(solution)/shard_map/pallas_call | solution.py:428
  132.8 1.9 %copy.11 = f32[192,768]{1,0:T(8,128)} copy(f32[192,768]{1,0:T(8,128)} %get-tuple-element.8) | data formatting | bytes 1179648
  134.7 1.9 %copy.12 = f32[1,192,768]{2,1,0:T(8,128)} copy(f32[1,192,768]{2,1,0:T(8,128)} %bitcast.5) | data formatting | bytes 1179648

commit v4 on v3

--- a/solution.py
+++ b/solution.py
@@ -34,13 +34,10 @@
 
 
 def product(ah, al, bh, bl, cols):
-    left_h, left_l = ah, al
-    rh, rl = bh[:, cols], bl[:, cols]
-    return jnp.dot(
-        jnp.concatenate([left_h, left_h, left_l], axis=1),
-        jnp.concatenate([rh, rl, rh], axis=0),
-        preferred_element_type=F32,
-    )
+    rows = ah.shape[0]
+    right = bh[:, cols]
+    both = jnp.dot(jnp.concatenate([ah, al], axis=0), right, preferred_element_type=F32)
+    return both[:rows] + (both[rows:] + jnp.dot(ah, bl[:, cols], preferred_element_type=F32))
 
 
 def wait(ref, sem):
@@ -190,8 +187,8 @@
     def gather_start(f):
         @pl.when(is_owner)
         def _():
-            for dz in range(2):
-                for dr in range(4):
+            for dr in (2, 1, 3, 0):
+                for dz in (1, 0):
                     tt, rr = term(cx, (zl + dz) % 2, cy, to_core), (r + dr) % 4
                     dst = ga.at[f, to_core, to_pos, to_slot]
                     if dz == 0 and dr == 0:
@@ -227,16 +224,17 @@
         for d in order:
             if d > 0:
                 wait(block(side_b, d), s1_recv.at[f, d - 1])
-            for n in (1, 3, 2):
+            for n in (1, 3) if d in (0, 1) else (1, 3, 2):
                 push(side_b, d, partner((side_b + n) % 4, side_a), 4 * (n - 1) + d)
             across(side_b, d, d)
         if after_push:
             after_push()
-        for n in (1, 3, 2):
-            for d in order:
-                bb = (side_b + 4 - n) % 4
-                wait(block(bb, d), s2_recv.at[f, 4 * (n - 1) + d])
-                across(bb, d, 4 * n + d)
+        for n, d in [(n, d) for d in order for n in (1, 3)] + [(2, d) for d in (0, 1, 3, 2)]:
+            bb = (side_b + 4 - n) % 4
+            wait(block(bb, d), s2_recv.at[f, 4 * (n - 1) + d])
+            if (n, d) in ((1, 0), (3, 1)):
+                push(bb, d, partner((side_b + n) % 4, side_a), 4 + d)
+            across(bb, d, 4 * n + d)
         for n in (0, 1, 3, 2):
             for d in order:
                 bb = (side_a + 4 - n) % 4
@@ -418,6 +416,17 @@
         wait(co.at[pl.ds(0, 63)], c2_send)
 
     wait(cf.at[pl.ds(0, 3 * SLAB)], c3_send)
+
+
+def hand_on(iso_in, env_in, iso_out, env_out, sem):
+    copies = [
+        pltpu.make_async_copy(iso_in, iso_out, sem.at[0]),
+        pltpu.make_async_copy(env_in, env_out, sem.at[1]),
+    ]
+    for copy in copies:
+        copy.start()
+    for copy in copies:
+        copy.wait()
 
 
 def body(amplitudes, left_terms, right_terms, source_list, list_count, weight_index, weight_table):
@@ -455,6 +464,15 @@
         amplitudes, left_terms.reshape(SLAB, K), right_terms.reshape(K, K),
         source_list.T, list_count, weight_index.T, weight_table,
     )
+    anywhere = pl.BlockSpec(memory_space=pl.ANY)
+    iso, env = pl.pallas_call(
+        hand_on,
+        out_shape=(slab, slab),
+        in_specs=[anywhere] * 2,
+        out_specs=(anywhere,) * 2,
+        scratch_shapes=[dma((2,))],
+        cost_estimate=pl.CostEstimate(flops=0, bytes_accessed=4 * SLAB * K * 4, transcendentals=0),
+    )(iso, env)
     return iso, env.reshape(1, SLAB, K)
 
 

time: 137 us -> 165 us (1.20)
  Pallas kernels: 132 us -> 164 us
  local copies, waits for them, and re-layouts: 3.83 us -> 0 us
    pallas_call x0 -> x1, Pallas kernels: none -> 36.9 us  [body(): pl.pallas_call(hand_on, out_shape=(slab, slab), in_specs=[anywhere] * 2,...]
    pallas_call x1, Pallas kernels: 132 us -> 127 us  [body(): pl.pallas_call(kernel, out_shape=(slab, slab), in_specs=[vmem] + [pl.Bloc...]
    unnamed x2 -> x0, local copies, waits for them, and re-layouts: 3.83 us -> none
where the time goes in v4:
time: 165 us
  Pallas kernels  164 us (99%)
    pallas_call x1, Pallas kernels, body(): pl.pallas_call(kernel, out_shape=(slab, slab), in_specs=[vmem] + [pl.Bloc...  127 us
    pallas_call x1, Pallas kernels, body(): pl.pallas_call(hand_on, out_shape=(slab, slab), in_specs=[anywhere] * 2,...  36.9 us

profile of v4, /device:TPU:1, one launch (start us, length us, event | category | flops | bytes accessed | tf_op | source)
XLA Modules:
  0.0 164.8 jit_solution(11522307693291334867)
XLA Ops:
  0.6 127.1 %shard_map.86 = (f32[192,768]{1,0:T(8,128)}, f32[192,768]{1,0:T(8,128)}) custom-call(f32[192,768]{1,0:T(8,128)} %a_ref.1, f32[192,768]{1,0:T(8,128)} %bitcast.6, f32[768,768]{1,0:T(8,128)} %bitcast.5, s32[4,64]{1,0:T(4,128)} %bitcast.8, s32[64]{0:T(128)} %count.1, s32[4,64]{1,0:T(4,128)} %bitcast.9, f32[8]{0:T(128)} %wtable.1), custom_call_target="tpu_custom_call" | custom-call | flops 28000000000 | bytes 8000000 | tf_op jit(solution)/shard_map/pallas_call | solution.py:437
  127.7 36.9 %shard_map.87 = (f32[192,768]{1,0:T(8,128)}, f32[192,768]{1,0:T(8,128)}) custom-call(f32[192,768]{1,0:T(8,128)} %get-tuple-element.6.iso_in, f32[192,768]{1,0:T(8,128)} %get-tuple-element.7.env_in), custom_call_target="tpu_custom_call" | custom-call | bytes 2359296 | tf_op jit(solution)/shard_map/pallas_call | solution.py:468

commit v5 on v4

--- a/solution.py
+++ b/solution.py
@@ -34,10 +34,13 @@
 
 
 def product(ah, al, bh, bl, cols):
+    return joined(ah, al, bh[:, cols], bl[:, cols])
+
+
+def joined(ah, al, bh, bl):
     rows = ah.shape[0]
-    right = bh[:, cols]
-    both = jnp.dot(jnp.concatenate([ah, al], axis=0), right, preferred_element_type=F32)
-    return both[:rows] + (both[rows:] + jnp.dot(ah, bl[:, cols], preferred_element_type=F32))
+    both = jnp.dot(jnp.concatenate([ah, al], axis=0), bh, preferred_element_type=F32)
+    return both[:rows] + (both[rows:] + jnp.dot(ah, bl, preferred_element_type=F32))
 
 
 def wait(ref, sem):
@@ -92,16 +95,17 @@
     bring_r.start()
     barrier = pltpu.get_barrier_semaphore()
 
-    @pl.loop(1, 64)
-    def _(i):
-        pl.semaphore_signal(barrier, inc=1, device_id=there((t + i) % 64, r), device_id_type=MESH)
-
-    for dr in range(1, 4):
+    for dr in (2, 1, 3):
         for zz in range(2):
             for cc in range(2):
                 pl.semaphore_signal(
                     barrier, inc=1, device_id=there(term(cx, zz, cy, cc), (r + dr) % 4), device_id_type=MESH
                 )
+
+    @pl.loop(1, 64)
+    def _(i):
+        pl.semaphore_signal(barrier, inc=1, device_id=there((t + i) % 64, r), device_id_type=MESH)
+
     bring_l.wait()
     split(l_ref, lh, ll, SLAB, 48)
     bring_r.wait()
@@ -266,12 +270,9 @@
                     chunk(x, m, (k % 4) * SLAB)[...] = ga[f, cc, s, i]
 
     def apply_terms(f):
-        split(x, xh, xl, K, 64)
-
-        @pl.loop(0, 3)
-        def _(n):
-            cols = pl.ds(pl.multiple_of(n * 256, 256), 256)
-            uh[:, cols], ul[:, cols] = halves(product(lh[...], ll[...], xh, xl, cols))
+        for n in range(3):
+            high, low = halves(x[:, tile(n)])
+            uh[:, tile(n)], ul[:, tile(n)] = halves(joined(lh[...], ll[...], high, low))
 
         for n in range(3):
             part[:, tile(n)] = product(uh[...], ul[...], rh, rl, tile(n))
@@ -387,9 +388,13 @@
     for sweep in range(SWEEPS):
         symmetric(yh, yl, now[0], now[1], gh, gl, lambda value, n: value)
         symmetric(gh, gl, gh, gl, wh, wl, polynomial)
+        if sweep == SWEEPS - 1:
+            for rr, hh, sem in ((ring_left, 1, 1), (ring_right, 0, 3), (ring_far, 0, 4), (ring_far, 1, 5)):
+                wait(slab_half(rr, hh), c3_recv.at[sem])
         for n in range(3):
             value = product(now[0][...], now[1][...], wh, wl, tile(n))
             if sweep == SWEEPS - 1:
+                gh[tile(n), :], gl[tile(n), :] = halves(cf[tile(n), :])
                 value = value * math.sqrt(K)
                 x[:, tile(n)] = value
             later[0][:, tile(n)], later[1][:, tile(n)] = halves(value)
@@ -398,9 +403,6 @@
 
     my_rows = pl.ds(pl.multiple_of(r * SLAB, SLAB), SLAB)
     iso_ref[...] = x[my_rows, :]
-    for rr, hh, sem in ((ring_left, 1, 1), (ring_right, 0, 3), (ring_far, 0, 4), (ring_far, 1, 5)):
-        wait(slab_half(rr, hh), c3_recv.at[sem])
-    split(cf, gh, gl, K, 64)
 
     for n in range(3):
         uh[:, tile(n)], ul[:, tile(n)] = halves(product(yh[my_rows, :], yl[my_rows, :], gh, gl, tile(n)))
@@ -418,15 +420,23 @@
     wait(cf.at[pl.ds(0, 3 * SLAB)], c3_send)
 
 
-def hand_on(iso_in, env_in, iso_out, env_out, sem):
-    copies = [
-        pltpu.make_async_copy(iso_in, iso_out, sem.at[0]),
-        pltpu.make_async_copy(env_in, env_out, sem.at[1]),
-    ]
-    for copy in copies:
-        copy.start()
-    for copy in copies:
-        copy.wait()
+def hand_on(iso_in, env_in, iso_out, env_out, buf, arrived, left):
+    pieces = []
+    for n, (src, dst) in enumerate(((iso_in, iso_out), (env_in, env_out))):
+        for m in range(2):
+            rows = pl.ds(96 * m, 96)
+            slot = 2 * n + m
+            pieces.append((
+                pltpu.make_async_copy(src.at[rows], buf.at[slot], arrived.at[slot]),
+                pltpu.make_async_copy(buf.at[slot], dst.at[rows], left.at[slot]),
+            ))
+    for come, _ in pieces:
+        come.start()
+    for come, go in pieces:
+        come.wait()
+        go.start()
+    for _, go in pieces:
+        go.wait()
 
 
 def body(amplitudes, left_terms, right_terms, source_list, list_count, weight_index, weight_table):
@@ -470,7 +480,7 @@
         out_shape=(slab, slab),
         in_specs=[anywhere] * 2,
         out_specs=(anywhere,) * 2,
-        scratch_shapes=[dma((2,))],
+        scratch_shapes=[pltpu.VMEM((4, 96, K), F32), dma((4,)), dma((4,))],
         cost_estimate=pl.CostEstimate(flops=0, bytes_accessed=4 * SLAB * K * 4, transcendentals=0),
     )(iso, env)
     return iso, env.reshape(1, SLAB, K)

time: 165 us -> 129 us (0.78)
  Pallas kernels: 164 us -> 128 us
    pallas_call x1, Pallas kernels: 36.9 us -> 2.04 us  [body(): pl.pallas_call(hand_on, out_shape=(slab, slab), in_specs=[anywhere] * 2,...]
where the time goes in v5:
time: 129 us
  Pallas kernels  128 us (99%)
    pallas_call x1, Pallas kernels, body(): pl.pallas_call(kernel, out_shape=(slab, slab), in_specs=[vmem] + [pl.Bloc...  126 us

profile of v5, /device:TPU:1, one launch (start us, length us, event | category | flops | bytes accessed | tf_op | source)
XLA Modules:
  0.0 129.2 jit_solution(15087406643889049790)
XLA Ops:
  0.6 126.3 %shard_map.86 = (f32[192,768]{1,0:T(8,128)}, f32[192,768]{1,0:T(8,128)}) custom-call(f32[192,768]{1,0:T(8,128)} %a_ref.1, f32[192,768]{1,0:T(8,128)} %bitcast.6, f32[768,768]{1,0:T(8,128)} %bitcast.5, s32[4,64]{1,0:T(4,128)} %bitcast.8, s32[64]{0:T(128)} %count.1, s32[4,64]{1,0:T(4,128)} %bitcast.9, f32[8]{0:T(128)} %wtable.1), custom_call_target="tpu_custom_call" | custom-call | flops 28000000000 | bytes 8000000 | tf_op jit(solution)/shard_map/pallas_call | solution.py:447
  126.9 2.0 %shard_map.87 = (f32[192,768]{1,0:T(8,128)}, f32[192,768]{1,0:T(8,128)}) custom-call(f32[192,768]{1,0:T(8,128)} %get-tuple-element.6.iso_in, f32[192,768]{1,0:T(8,128)} %get-tuple-element.7.env_in), custom_call_target="tpu_custom_call" | custom-call | bytes 2359296 | tf_op jit(solution)/shard_map/pallas_call | solution.py:478

commit v6 on v5

--- a/solution.py
+++ b/solution.py
@@ -228,7 +228,7 @@
         for d in order:
             if d > 0:
                 wait(block(side_b, d), s1_recv.at[f, d - 1])
-            for n in (1, 3) if d in (0, 1) else (1, 3, 2):
+            for n in (1, 3):
                 push(side_b, d, partner((side_b + n) % 4, side_a), 4 * (n - 1) + d)
             across(side_b, d, d)
         if after_push:
@@ -236,7 +236,7 @@
         for n, d in [(n, d) for d in order for n in (1, 3)] + [(2, d) for d in (0, 1, 3, 2)]:
             bb = (side_b + 4 - n) % 4
             wait(block(bb, d), s2_recv.at[f, 4 * (n - 1) + d])
-            if (n, d) in ((1, 0), (3, 1)):
+            if (n, d) in ((1, 0), (3, 1), (1, 3), (3, 2)):
                 push(bb, d, partner((side_b + n) % 4, side_a), 4 + d)
             across(bb, d, 4 * n + d)
         for n in (0, 1, 3, 2):

time: 129 us -> 129 us (level)
  no operation moved by 1% of the time
where the time goes in v6:
time: 129 us
  Pallas kernels  128 us (99%)
    pallas_call x1, Pallas kernels, body(): pl.pallas_call(kernel, out_shape=(slab, slab), in_specs=[vmem] + [pl.Bloc...  126 us

profile of v6, /device:TPU:1, one launch (start us, length us, event | category | flops | bytes accessed | tf_op | source)
XLA Modules:
  0.0 128.6 jit_solution(5921840553248090034)
XLA Ops:
  0.6 125.7 %shard_map.86 = (f32[192,768]{1,0:T(8,128)}, f32[192,768]{1,0:T(8,128)}) custom-call(f32[192,768]{1,0:T(8,128)} %a_ref.1, f32[192,768]{1,0:T(8,128)} %bitcast.6, f32[768,768]{1,0:T(8,128)} %bitcast.5, s32[4,64]{1,0:T(4,128)} %bitcast.8, s32[64]{0:T(128)} %count.1, s32[4,64]{1,0:T(4,128)} %bitcast.9, f32[8]{0:T(128)} %wtable.1), custom_call_target="tpu_custom_call" | custom-call | flops 28000000000 | bytes 8000000 | tf_op jit(solution)/shard_map/pallas_call | solution.py:447
  126.4 2.0 %shard_map.87 = (f32[192,768]{1,0:T(8,128)}, f32[192,768]{1,0:T(8,128)}) custom-call(f32[192,768]{1,0:T(8,128)} %get-tuple-element.6.iso_in, f32[192,768]{1,0:T(8,128)} %get-tuple-element.7.env_in), custom_call_target="tpu_custom_call" | custom-call | bytes 2359296 | tf_op jit(solution)/shard_map/pallas_call | solution.py:478
